TPU v7x, 32 devices: a whole 2x2x4 slice. The times are simulated.
32 devices in a mesh: district: 2 (over x), tile: 16 (over z, y, core).
Axes of the slice: x: 2, y: 2, z: 4, core: 2. Of those that a mesh axis runs over, the one named last changes fastest.
Arguments:
- cotangent: bfloat16 [384, 49152], P('tile', 'district'), parts along dimension 1, may hold values from -6 to 6
- coeffs: bfloat16 [2305, 49152], P(None, ('district', 'tile')), parts along dimension 1, may hold values from -0.0390625 to 0.0390625
- ctf: float32 [8, 24], replicated, may hold values from -1.5 to 1.5
- tap_count: int32 [8], replicated, may hold values from 1 to 24, as said below
- construction: int32 [49152], P('district'), parts along dimension 0, may hold values from 0 to 7
Outputs:
- sky_grad: float32 [384, 4610], P('tile', 'district'), parts along dimension 1
There are 2 independent parts, one for each index of `district`. A program takes and returns all parts, laid end to end along the dimension named above; an argument that names none is the same for every part. Nothing has to cross between parts.
Inputs may be any that keep to these rules, and one draw needn't show every extreme that they name: `tap_count`: some type has 24 live taps and some has one.
All inputs are finite; a program needn't handle non-finite values.
Results may differ from a plain program's by a relative error of at most 0.0029.
Values may be sent and summed in bfloat16 or wider, within the bound.
A program may use at most 128 MiB of HBM per device.

v0:
```python
import jax
import jax.numpy as jnp
from jax import lax
from jax.sharding import PartitionSpec as P


def shifted(value, axis, by):
    size = lax.axis_size(axis)
    pairs = [(i, i + by) for i in range(size) if 0 <= i + by < size]
    return lax.ppermute(value, axis, pairs)


def taps_table(kinds, tap_count, ctf):
    onehot = (kinds[:, None] == jnp.arange(ctf.shape[0], dtype=jnp.int32)[None, :]).astype(
        jnp.float32
    )
    live = jnp.where(
        jnp.arange(ctf.shape[1], dtype=jnp.int32)[None, :] < tap_count[:, None],
        ctf,
        jnp.float32(0.0),
    )
    return jnp.einsum("sc,ck->ks", onehot, live, precision=lax.Precision.HIGHEST)


def correlate(extended, taps, length):
    accum = jnp.zeros((length, extended.shape[1]), jnp.float32)
    for shift_k in range(taps.shape[0]):
        accum = accum + taps[shift_k][None, :] * extended[shift_k : shift_k + length].astype(
            jnp.float32
        )
    return accum.astype(jnp.bfloat16)


def per_device(cotangent, coeffs, ctf, tap_count, construction):
    span = ctf.shape[1]
    hours = cotangent.shape[0]
    taps = taps_table(construction, tap_count, ctf)
    tail = shifted(cotangent[: span - 1], "tile", -1)
    extended = jnp.concatenate([cotangent, tail], 0)
    surface = correlate(extended, taps, hours)
    by_points = lax.all_to_all(surface, "tile", split_axis=1, concat_axis=0, tiled=True)
    partial_value = lax.dot_general(
        by_points, coeffs, (((1,), (1,)), ((), ())), preferred_element_type=jnp.float32
    )
    return lax.psum_scatter(partial_value, "tile", scatter_dimension=0, tiled=True)


def solution(mesh):
    return jax.shard_map(
        per_device,
        mesh=mesh,
        in_specs=(P("tile", "district"), P(None, ("district", "tile")), P(), P(), P("district")),
        out_specs=P("tile", "district"),
        check_vma=False,
    )
```

profile of v0, /device:TPU:0, one launch (start us, length us, event | category | flops | bytes accessed | tf_op | source)
XLA Modules:
  0.0 148.4 jit_solution(18111956519017167114)
XLA Ops:
  6.5 0.0 reduce-scatter.4.cloned.1.call-start
  6.5 1.3 collective-permute-start
  7.8 2.1 %fusion = f32[24,24576]{1,0:T(8,128)S(1)} fusion(s32[24576]{0:T(1024)} %param.9, f32[8,24]{1,0:T(8,128)} %param.7, s32[8]{0:T(128)} %param.8), kind=kOutput, calls=%fused_computation.3 | convolution fusion | flops 56820096 | bytes 2458400 | tf_op jit(solution)/shard_map/sc,ck->ks/dot_general | solution.py:22
  9.9 0.0 copy-start
  10.0 1.6 %fusion.6 = (f32[1,24576]{1,0:T(1,128)S(1)}, f32[1,24576]{1,0:T(1,128)S(1)}, f32[1,24576]{1,0:T(1,128)S(1)}, f32[1,24576]{1,0:T(1,128)S(1)}, f32[1,24576]{1,0:T(...) fusion(f32[24,24576]{1,0:T(8,128)S(1)} %fusion), kind=kLoop, calls=%fused_computation.12 | loop fusion | bytes 3735552 | tf_op jit(solution)/shard_map/slice | solution.py:28
  11.6 0.4 fusion.7
  12.0 0.0 copy-done
  12.0 0.1 constant_dynamic-update-slice_fusion.1
  12.0 0.0 collective-permute-done
  12.1 0.0 slice-start
  12.1 0.1 constant_dynamic-update-slice_fusion
  12.2 0.0 slice-start.1
  12.2 7.4 %add_convert_fusion = bf16[24,24576]{1,0:T(8,128)(2,1)S(1)} fusion(bf16[24,24576]{1,0:T(8,128)(2,1)S(1)} %copy-done, bf16[47,24576]{1,0:T(8,128)(2,1)S(1)} %constant_dynamic-update-slice_fusion, f32[24576]{0:T(1024)S(1)} %bitcast.40, f32[24576]{0:T(1024)S(1)} %bitcast.41, f32[24576]{0:T(1024)S(1)} %bitcast.42, f32[24576]{0:T(1024)S(1)} %bitcast.43, ...), kind=kLoop, calls=%fused_computation | loop fusion | flops 42467328 | bytes 31850496 | tf_op jit(solution)/shard_map/convert_element_type | solution.py:31
  19.6 0.1 copy.11
  19.7 48.2 %all_to_all.19 = bf16[24,16,1536]{2,0,1:T(8,128)(2,1)S(1)} all-to-all(bf16[24,16,1536]{2,0,1:T(8,128)(2,1)S(1)} %bitcast.37), channel_id=1, replica_groups=mesh['district'=2,'tile'=16] {'tile'}, dimensions={1} | all-to-all | bytes 2359296 | tf_op jit(solution)/shard_map/all_to_all | solution.py:41
  67.9 0.0 slice-done
  67.9 0.0 slice-done.1
  67.9 5.1 %fusion.8 = f32[384,2305]{1,0:T(8,128)} fusion(bf16[384,1536]{1,0:T(8,128)(2,1)S(1)} %bitcast.38, bf16[2305,1536]{1,0:T(8,128)(2,1)S(1)} %bitcast.64), kind=kOutput, calls=%fused_computation.14 | convolution fusion | flops 2719088640 | bytes 11801088 | tf_op jit(solution)/shard_map/dot_general | solution.py:42
  72.9 0.0 reduce-scatter.4.cloned.1.call-update
  73.0 68.6 %reduce-scatter.4.cloned.1.call-done = f32[24,2305]{1,0:T(8,128)} async-done(((f32[384,2305]{1,0:T(8,128)}), f32[24,2305]{1,0:T(8,128)}) %reduce-scatter.4.cloned.1.call-update) | async-done | bytes 221296
  (1 shorter events, 0.0 us)
Async XLA Ops:
  6.5 135.0 %reduce-scatter.4.cloned.1.call-start = ((), (), s32[]{:S(2)}) async-start(), calls=%async_computation.2 | async-start | bytes 3969024
  6.5 5.5 %collective-permute-start = (bf16[23,24576]{1,0:T(8,128)(2,1)}, bf16[23,24576]{1,0:T(8,128)(2,1)S(1)}, u32[]{:S(2)}, u32[]{:S(2)}) collective-permute-start(bf16[23,24576]{1,0:T(8,128)(2,1)} %bitcast.35), channel_id=1, source_target_pairs={{1,0},{2,1},{3,2},{4,3},{5,4},{6,5},{7,6},{8,7},{9,8},{10,9},{11,1... | collective-permute-start | bytes 3391496 | tf_op jit(solution)/shard_map/ppermute | solution.py:10
  9.9 2.0 %copy-start = (bf16[24,24576]{1,0:T(8,128)(2,1)S(1)}, bf16[24,24576]{1,0:T(8,128)(2,1)}, u32[]{:S(2)}) copy-start(bf16[24,24576]{1,0:T(8,128)(2,1)} %param.5) | copy-start | bytes 3538948
  12.1 55.8 %slice-start = ((s8[7102464]{0:T(1024)(128)(4,1)}), s8[4194304]{0:T(1024)(128)(4,1)S(1)}, s32[]{:S(2)}) async-start(s8[7102464]{0:T(1024)(128)(4,1)} %bitcast.63), calls=%async_computation.3 | async-start | bytes 8388608
  12.2 55.7 %slice-start.1 = ((s8[7102464]{0:T(1024)(128)(4,1)}), s8[2908160]{0:T(1024)(128)(4,1)S(1)}, s32[]{:S(2)}) async-start(s8[7102464]{0:T(1024)(128)(4,1)} %bitcast.63), calls=%async_computation.4 | async-start | bytes 5816320
Sparse Core Ops, SparseCore 0:
  73.1 68.3 reduce-scatter.3
where the time goes:
time: 149 us; the launch traced here: 148 us
  waiting for transfers between devices  68.6 us (46%)
  blocking collectives  48.2 us (32%)
  between operations  13.5 us (9%)
  other arithmetic  7.44 us (5%)
  matrix products  7.16 us (5%)
  local copies, waits for them, and re-layouts  2.24 us (2%)
    unnamed x2, waiting for transfers between devices  68.6 us
    all_to_all x1, blocking collectives, per_device(): lax.all_to_all(surface, 'tile', split_axis=1, concat_axis=0, tiled=True)  48.2 us
    convert_element_type x1, other arithmetic, correlate(): return accum.astype(jnp.bfloat16)  7.44 us
    dot_general x1, matrix products, per_device(): lax.dot_general(by_points, coeffs, (((1,), (1,)), ((), ())), preferred_el...  5.05 us
  transfers between devices with their start and end apart: 2, of which 1 were waited for; matrix products, arithmetic and copies ran while one was open for 3% of the time, Pallas kernels for 0%

commit v1 on v0

--- a/solution.py
+++ b/solution.py
@@ -2,6 +2,24 @@
 import jax.numpy as jnp
 from jax import lax
 from jax.sharding import PartitionSpec as P
+
+
+def perform_view_up(local_values, mesh_name):
+    arr_out, z = (jax.lax.axis_size(mesh_name), jax.lax.axis_index(mesh_name))
+    formed = local_values.shape[1] // arr_out
+    value_now = list(local_values.shape)
+    value_now[1] = formed
+    n_now = value_now[0]
+    value_now[0] = n_now * arr_out
+    x_now = jnp.zeros(value_now, local_values.dtype)
+    for no in range(arr_out):
+        u_next = lax.dynamic_slice_in_dim(local_values, (z ^ no) * formed, formed, axis=1)
+        if no:
+            u_next = jax.lax.ppermute(
+                u_next, mesh_name, tuple(((k, k ^ no) for k in range(arr_out)))
+            )
+        x_now = lax.dynamic_update_slice_in_dim(x_now, u_next, (z ^ no) * n_now, axis=0)
+    return x_now
 
 
 def shifted(value, axis, by):
@@ -38,7 +56,7 @@
     tail = shifted(cotangent[: span - 1], "tile", -1)
     extended = jnp.concatenate([cotangent, tail], 0)
     surface = correlate(extended, taps, hours)
-    by_points = lax.all_to_all(surface, "tile", split_axis=1, concat_axis=0, tiled=True)
+    by_points = perform_view_up(surface, "tile")
     partial_value = lax.dot_general(
         by_points, coeffs, (((1,), (1,)), ((), ())), preferred_element_type=jnp.float32
     )

time: 149 us -> 156 us (1.047)
  blocking collectives: 48.2 us -> 0 us
  starting transfers between devices: 1.28 us -> 40 us
  waiting for transfers between devices: 68.6 us -> 78.8 us
  local copies, waits for them, and re-layouts: 2.24 us -> 5.63 us
  matrix products: 7.16 us -> 10.2 us
    all_to_all x1 -> x0, blocking collectives: 48.2 us -> none  [per_device(): lax.all_to_all(surface, 'tile', split_axis=1, concat_axis=0, tiled=True)]
    ppermute x0 -> x15, starting transfers between devices: none -> 38.7 us  [perform_view_up(): jax.lax.ppermute(u_next, mesh_name, tuple(((k, k ^ no) for k in range(arr...]
    ppermute x0 -> x15, waiting for transfers between devices: none -> 7.34 us  [perform_view_up(): jax.lax.ppermute(u_next, mesh_name, tuple(((k, k ^ no) for k in range(arr...]
    dot_general x1, matrix products: 5.05 us -> 8.1 us  [per_device(): lax.dot_general(by_points, coeffs, (((1,), (1,)), ((), ())), preferred_el...]
    unnamed x2, waiting for transfers between devices: 68.6 us -> 71.4 us
  transfers between devices with their start and end apart: 2 -> 17, of which waited for: 1 -> 5; matrix products, arithmetic and copies ran while one was open for 3% -> 4% of each run, Pallas kernels for 0% -> 0%
where the time goes in v1:
time: 156 us
  waiting for transfers between devices  78.8 us (51%)
  starting transfers between devices  40 us (26%)
  between operations  14.1 us (9%)
  matrix products  10.2 us (7%)
  other arithmetic  7.42 us (5%)
  local copies, waits for them, and re-layouts  5.63 us (4%)
    unnamed x2, waiting for transfers between devices  71.4 us
    ppermute x15, starting transfers between devices, perform_view_up(): jax.lax.ppermute(u_next, mesh_name, tuple(((k, k ^ no) for k in range(arr...  38.7 us
    dot_general x1, matrix products, per_device(): lax.dot_general(by_points, coeffs, (((1,), (1,)), ((), ())), preferred_el...  8.1 us
    convert_element_type x1, other arithmetic, correlate(): return accum.astype(jnp.bfloat16)  7.42 us
    ppermute x15, waiting for transfers between devices, perform_view_up(): jax.lax.ppermute(u_next, mesh_name, tuple(((k, k ^ no) for k in range(arr...  7.34 us
    slice x2, local copies, waits for them, and re-layouts, correlate(): taps[shift_k][None, :]  3.46 us
  transfers between devices with their start and end apart: 17, of which 5 were waited for; matrix products, arithmetic and copies ran while one was open for 4% of the time, Pallas kernels for 0%

profile of v1, /device:TPU:0, one launch (start us, length us, event | category | flops | bytes accessed | tf_op | source)
XLA Modules:
  0.0 156.1 jit_solution(6899491524709529267)
XLA Ops:
  6.5 1.3 collective-permute-start
  7.8 2.1 %fusion = f32[24,24576]{1,0:T(8,128)S(1)} fusion(s32[24576]{0:T(1024)} %param.9, f32[8,24]{1,0:T(8,128)} %param.7, s32[8]{0:T(128)} %param.8), kind=kOutput, calls=%fused_computation.2 | convolution fusion | flops 56820096 | bytes 2458400 | tf_op jit(solution)/shard_map/sc,ck->ks/dot_general | solution.py:40
  9.9 0.0 copy-start
  10.0 2.3 %fusion.6 = (f32[1,24576]{1,0:T(1,128)}, f32[1,24576]{1,0:T(1,128)}, f32[1,24576]{1,0:T(1,128)}, f32[1,24576]{1,0:T(1,128)}, f32[1,24576]{1,0:T(1,128)}, /*index...) fusion(f32[24,24576]{1,0:T(8,128)S(1)} %fusion), kind=kLoop, calls=%fused_computation.42 | loop fusion | bytes 3735552 | tf_op jit(solution)/shard_map/slice | solution.py:46
  12.3 1.2 fusion.7
  13.4 0.1 constant_dynamic-update-slice_fusion.16
  13.6 0.0 copy-start.1
  13.8 0.0 collective-permute-done
  13.9 1.6 %constant_dynamic-update-slice_fusion.15 = bf16[47,24576]{1,0:T(8,128)(2,1)S(1)} fusion(bf16[47,24576]{1,0:T(8,128)(2,1)S(1)} %constant_dynamic-update-slice_fusion.16, bf16[23,24576]{1,0:T(8,128)(2,1)} %collective-permute-done), kind=kLoop, calls=%fused_computation.35 | loop fusion | bytes 2310144 | tf_op jit(solution)/shard_map/concatenate | solution.py:57
  15.4 0.0 copy-done.1
  15.7 0.0 copy-done.23
  15.7 0.0 copy-done.24
  15.7 7.4 %add_convert_fusion = bf16[24,24576]{1,0:T(8,128)(2,1)S(1)} fusion(bf16[24,24576]{1,0:T(8,128)(2,1)S(1)} %copy-done, bf16[47,24576]{1,0:T(8,128)(2,1)S(1)} %constant_dynamic-update-slice_fusion.15, f32[24576]{0:T(1024)S(1)} %bitcast.30, f32[24576]{0:T(1024)S(1)} %bitcast.31, f32[24576]{0:T(1024)S(1)} %bitcast.32, f32[24576]{0:T(1024)S(1)} %bitcast.33, ...), kind=kLoop, calls=%fused_computation | loop fusion | flops 42467328 | bytes 31850496 | tf_op jit(solution)/shard_map/convert_element_type | solution.py:49
  23.1 0.1 broadcast_in_dim.5
  23.2 0.2 constant_dynamic-slice_fusion
  23.4 11.7 %collective-permute-start.1 = (bf16[24,1536]{1,0:T(8,128)(2,1)S(1)}, bf16[24,1536]{1,0:T(8,128)(2,1)S(1)}, u32[]{:S(2)}, u32[]{:S(2)}) collective-permute-start(bf16[24,1536]{1,0:T(8,128)(2,1)S(1)} %get-tuple-element.43), channel_id=1, source_target_pairs={{0,1},{1,0},{2,3},{3,2},{4,5},{5,4},{6,7},{7,6},{8,9},{9,8},{10,11... | collective-permute-start | bytes 221192 | tf_op jit(solution)/shard_map/ppermute | solution.py:18
  35.1 2.4 %collective-permute-start.2 = (bf16[24,1536]{1,0:T(8,128)(2,1)S(1)}, bf16[24,1536]{1,0:T(8,128)(2,1)S(1)}, u32[]{:S(2)}, u32[]{:S(2)}) collective-permute-start(bf16[24,1536]{1,0:T(8,128)(2,1)S(1)} %get-tuple-element.42), channel_id=1, source_target_pairs={{0,2},{1,3},{2,0},{3,1},{4,6},{5,7},{6,4},{7,5},{8,10},{9,11},{10,... | collective-permute-start | bytes 221192 | tf_op jit(solution)/shard_map/ppermute | solution.py:18
  37.4 0.0 collective-permute-start.3
  37.4 1.6 %collective-permute-start.4 = (bf16[24,1536]{1,0:T(8,128)(2,1)S(1)}, bf16[24,1536]{1,0:T(8,128)(2,1)S(1)}, u32[]{:S(2)}, u32[]{:S(2)}) collective-permute-start(bf16[24,1536]{1,0:T(8,128)(2,1)S(1)} %get-tuple-element.40), channel_id=1, source_target_pairs={{0,4},{1,5},{2,6},{3,7},{4,0},{5,1},{6,2},{7,3},{8,12},{9,13},{10,... | collective-permute-start | bytes 221192 | tf_op jit(solution)/shard_map/ppermute | solution.py:18
  39.0 0.0 collective-permute-start.5
  39.0 0.0 collective-permute-done.1
  39.0 2.9 %collective-permute-start.6 = (bf16[24,1536]{1,0:T(8,128)(2,1)S(1)}, bf16[24,1536]{1,0:T(8,128)(2,1)S(1)}, u32[]{:S(2)}, u32[]{:S(2)}) collective-permute-start(bf16[24,1536]{1,0:T(8,128)(2,1)S(1)} %get-tuple-element.38), channel_id=1, source_target_pairs={{0,6},{1,7},{2,4},{3,5},{4,2},{5,3},{6,0},{7,1},{8,14},{9,15},{10,... | collective-permute-start | bytes 221192 | tf_op jit(solution)/shard_map/ppermute | solution.py:18
  42.0 0.0 collective-permute-done.2
  42.0 0.1 collective-permute-start.7
  42.1 0.0 collective-permute-done.3
  42.1 2.5 %collective-permute-start.8 = (bf16[24,1536]{1,0:T(8,128)(2,1)S(1)}, bf16[24,1536]{1,0:T(8,128)(2,1)S(1)}, u32[]{:S(2)}, u32[]{:S(2)}) collective-permute-start(bf16[24,1536]{1,0:T(8,128)(2,1)S(1)} %get-tuple-element.36), channel_id=1, source_target_pairs={{0,8},{1,9},{2,10},{3,11},{4,12},{5,13},{6,14},{7,15},{8,0},{9,1},... | collective-permute-start | bytes 221192 | tf_op jit(solution)/shard_map/ppermute | solution.py:18
  44.6 0.0 collective-permute-done.4
  44.6 1.5 collective-permute-start.9
  46.1 0.0 collective-permute-done.5
  46.1 2.5 %collective-permute-start.10 = (bf16[24,1536]{1,0:T(8,128)(2,1)S(1)}, bf16[24,1536]{1,0:T(8,128)(2,1)S(1)}, u32[]{:S(2)}, u32[]{:S(2)}) collective-permute-start(bf16[24,1536]{1,0:T(8,128)(2,1)S(1)} %get-tuple-element.34), channel_id=1, source_target_pairs={{0,10},{1,11},{2,8},{3,9},{4,14},{5,15},{6,12},{7,13},{8,2},{9,3},... | collective-permute-start | bytes 221192 | tf_op jit(solution)/shard_map/ppermute | solution.py:18
  48.6 0.0 collective-permute-done.6
  48.6 0.1 collective-permute-start.11
  48.7 0.5 collective-permute-done.7
  49.2 2.8 %collective-permute-start.12 = (bf16[24,1536]{1,0:T(8,128)(2,1)S(1)}, bf16[24,1536]{1,0:T(8,128)(2,1)S(1)}, u32[]{:S(2)}, u32[]{:S(2)}) collective-permute-start(bf16[24,1536]{1,0:T(8,128)(2,1)S(1)} %get-tuple-element.32), channel_id=1, source_target_pairs={{0,12},{1,13},{2,14},{3,15},{4,8},{5,9},{6,10},{7,11},{8,4},{9,5},... | collective-permute-start | bytes 221192 | tf_op jit(solution)/shard_map/ppermute | solution.py:18
  52.0 0.0 collective-permute-done.8
  52.0 6.6 %collective-permute-start.13 = (bf16[24,1536]{1,0:T(8,128)(2,1)S(1)}, bf16[24,1536]{1,0:T(8,128)(2,1)S(1)}, u32[]{:S(2)}, u32[]{:S(2)}) collective-permute-start(bf16[24,1536]{1,0:T(8,128)(2,1)S(1)} %get-tuple-element.31), channel_id=1, source_target_pairs={{0,13},{1,12},{2,15},{3,14},{4,9},{5,8},{6,11},{7,10},{8,5},{9,4},... | collective-permute-start | bytes 221192 | tf_op jit(solution)/shard_map/ppermute | solution.py:18
  58.5 0.0 collective-permute-done.9
  58.6 3.3 %collective-permute-start.14 = (bf16[24,1536]{1,0:T(8,128)(2,1)S(1)}, bf16[24,1536]{1,0:T(8,128)(2,1)S(1)}, u32[]{:S(2)}, u32[]{:S(2)}) collective-permute-start(bf16[24,1536]{1,0:T(8,128)(2,1)S(1)} %get-tuple-element.30), channel_id=1, source_target_pairs={{0,14},{1,15},{2,12},{3,13},{4,10},{5,11},{6,8},{7,9},{8,6},{9,7},... | collective-permute-start | bytes 221192 | tf_op jit(solution)/shard_map/ppermute | solution.py:18
  61.9 0.6 collective-permute-done.10
  62.5 0.9 collective-permute-start.15
  63.4 0.0 collective-permute-done.11
  63.4 0.0 collective-permute-done.12
  63.5 0.0 collective-permute-done.13
  63.5 2.3 %collective-permute-done.14 = bf16[24,1536]{1,0:T(8,128)(2,1)S(1)} collective-permute-done((bf16[24,1536]{1,0:T(8,128)(2,1)S(1)}, bf16[24,1536]{1,0:T(8,128)(2,1)S(1)}, u32[]{:S(2)}, u32[]{:S(2)}) %collective-permute-start.14) | collective-permute-done | bytes 73760 | tf_op jit(solution)/shard_map/ppermute | solution.py:18
  65.8 3.9 %collective-permute-done.15 = bf16[24,1536]{1,0:T(8,128)(2,1)S(1)} collective-permute-done((bf16[24,1536]{1,0:T(8,128)(2,1)S(1)}, bf16[24,1536]{1,0:T(8,128)(2,1)S(1)}, u32[]{:S(2)}, u32[]{:S(2)}) %collective-permute-start.15) | collective-permute-done | bytes 73760 | tf_op jit(solution)/shard_map/ppermute | solution.py:18
  69.7 8.1 %fusion.8 = f32[384,2305]{1,0:T(8,128)} fusion(bf16[384,1536]{1,0:T(8,128)(2,1)S(1)} %constant_dynamic-update-slice_fusion.14, bf16[2305,1536]{1,0:T(8,128)(2,1)} %param.6), kind=kOutput, calls=%fused_computation.44 | convolution fusion | flops 2719088640 | bytes 11801088 | tf_op jit(solution)/shard_map/dot_general | solution.py:60
  77.8 0.0 reduce-scatter.4.cloned.1.call-update
  77.9 71.4 %reduce-scatter.4.cloned.1.call-done = f32[24,2305]{1,0:T(8,128)} async-done(((f32[384,2305]{1,0:T(8,128)}), f32[24,2305]{1,0:T(8,128)}) %reduce-scatter.4.cloned.1.call-update) | async-done | bytes 221296
  (61 shorter events, 0.2 us)
Async XLA Ops:
  6.5 142.8 %reduce-scatter.4.cloned.1.call-start = ((), (), s32[]{:S(2)}) async-start(), calls=%async_computation.1 | async-start | bytes 3969024
  6.5 7.3 %collective-permute-start = (bf16[23,24576]{1,0:T(8,128)(2,1)}, bf16[23,24576]{1,0:T(8,128)(2,1)}, u32[]{:S(2)}, u32[]{:S(2)}) collective-permute-start(bf16[23,24576]{1,0:T(8,128)(2,1)} %bitcast.28), channel_id=1, source_target_pairs={{1,0},{2,1},{3,2},{4,3},{5,4},{6,5},{7,6},{8,7},{9,8},{10,9},{11,1... | collective-permute-start | bytes 3391496 | tf_op jit(solution)/shard_map/ppermute | solution.py:28
  9.9 3.5 %copy-start = (bf16[24,24576]{1,0:T(8,128)(2,1)S(1)}, bf16[24,24576]{1,0:T(8,128)(2,1)}, u32[]{:S(2)}) copy-start(bf16[24,24576]{1,0:T(8,128)(2,1)} %param.5) | copy-start | bytes 3538948
  13.6 1.8 %copy-start.1 = (f32[1,24576]{1,0:T(1,128)S(1)}, f32[1,24576]{1,0:T(1,128)}, u32[]{:S(2)}) copy-start(f32[1,24576]{1,0:T(1,128)} %get-tuple-element.5) | copy-start | bytes 294916
  13.6 1.8 %copy-start.2 = (f32[1,24576]{1,0:T(1,128)S(1)}, f32[1,24576]{1,0:T(1,128)}, u32[]{:S(2)}) copy-start(f32[1,24576]{1,0:T(1,128)} %get-tuple-element.6) | copy-start | bytes 294916
  13.6 1.8 %copy-start.3 = (f32[1,24576]{1,0:T(1,128)S(1)}, f32[1,24576]{1,0:T(1,128)}, u32[]{:S(2)}) copy-start(f32[1,24576]{1,0:T(1,128)} %get-tuple-element.7) | copy-start | bytes 294916
  13.6 1.8 %copy-start.4 = (f32[1,24576]{1,0:T(1,128)S(1)}, f32[1,24576]{1,0:T(1,128)}, u32[]{:S(2)}) copy-start(f32[1,24576]{1,0:T(1,128)} %get-tuple-element.8) | copy-start | bytes 294916
  13.6 1.8 %copy-start.5 = (f32[1,24576]{1,0:T(1,128)S(1)}, f32[1,24576]{1,0:T(1,128)}, u32[]{:S(2)}) copy-start(f32[1,24576]{1,0:T(1,128)} %get-tuple-element.9) | copy-start | bytes 294916
  13.7 1.8 %copy-start.6 = (f32[1,24576]{1,0:T(1,128)S(1)}, f32[1,24576]{1,0:T(1,128)}, u32[]{:S(2)}) copy-start(f32[1,24576]{1,0:T(1,128)} %get-tuple-element.10) | copy-start | bytes 294916
  13.7 1.8 %copy-start.7 = (f32[1,24576]{1,0:T(1,128)S(1)}, f32[1,24576]{1,0:T(1,128)}, u32[]{:S(2)}) copy-start(f32[1,24576]{1,0:T(1,128)} %get-tuple-element.11) | copy-start | bytes 294916
  13.7 1.8 %copy-start.8 = (f32[1,24576]{1,0:T(1,128)S(1)}, f32[1,24576]{1,0:T(1,128)}, u32[]{:S(2)}) copy-start(f32[1,24576]{1,0:T(1,128)} %get-tuple-element.12) | copy-start | bytes 294916
  13.7 1.8 %copy-start.9 = (f32[1,24576]{1,0:T(1,128)S(1)}, f32[1,24576]{1,0:T(1,128)}, u32[]{:S(2)}) copy-start(f32[1,24576]{1,0:T(1,128)} %get-tuple-element.13) | copy-start | bytes 294916
  13.7 1.8 %copy-start.10 = (f32[1,24576]{1,0:T(1,128)S(1)}, f32[1,24576]{1,0:T(1,128)}, u32[]{:S(2)}) copy-start(f32[1,24576]{1,0:T(1,128)} %get-tuple-element.14) | copy-start | bytes 294916
  13.7 1.8 %copy-start.11 = (f32[1,24576]{1,0:T(1,128)S(1)}, f32[1,24576]{1,0:T(1,128)}, u32[]{:S(2)}) copy-start(f32[1,24576]{1,0:T(1,128)} %get-tuple-element.15) | copy-start | bytes 294916
  13.7 1.8 %copy-start.12 = (f32[1,24576]{1,0:T(1,128)S(1)}, f32[1,24576]{1,0:T(1,128)}, u32[]{:S(2)}) copy-start(f32[1,24576]{1,0:T(1,128)} %get-tuple-element.16) | copy-start | bytes 294916
  13.7 1.8 %copy-start.13 = (f32[1,24576]{1,0:T(1,128)S(1)}, f32[1,24576]{1,0:T(1,128)}, u32[]{:S(2)}) copy-start(f32[1,24576]{1,0:T(1,128)} %get-tuple-element.17) | copy-start | bytes 294916
  13.7 1.8 %copy-start.14 = (f32[1,24576]{1,0:T(1,128)S(1)}, f32[1,24576]{1,0:T(1,128)}, u32[]{:S(2)}) copy-start(f32[1,24576]{1,0:T(1,128)} %get-tuple-element.18) | copy-start | bytes 294916
  13.7 1.8 %copy-start.15 = (f32[1,24576]{1,0:T(1,128)S(1)}, f32[1,24576]{1,0:T(1,128)}, u32[]{:S(2)}) copy-start(f32[1,24576]{1,0:T(1,128)} %get-tuple-element.19) | copy-start | bytes 294916
  13.8 1.8 %copy-start.16 = (f32[1,24576]{1,0:T(1,128)S(1)}, f32[1,24576]{1,0:T(1,128)}, u32[]{:S(2)}) copy-start(f32[1,24576]{1,0:T(1,128)} %get-tuple-element.20) | copy-start | bytes 294916
  13.8 1.8 %copy-start.17 = (f32[1,24576]{1,0:T(1,128)S(1)}, f32[1,24576]{1,0:T(1,128)}, u32[]{:S(2)}) copy-start(f32[1,24576]{1,0:T(1,128)} %get-tuple-element.21) | copy-start | bytes 294916
  13.8 1.8 %copy-start.18 = (f32[1,24576]{1,0:T(1,128)S(1)}, f32[1,24576]{1,0:T(1,128)}, u32[]{:S(2)}) copy-start(f32[1,24576]{1,0:T(1,128)} %get-tuple-element.22) | copy-start | bytes 294916
  13.8 1.8 %copy-start.19 = (f32[1,24576]{1,0:T(1,128)S(1)}, f32[1,24576]{1,0:T(1,128)}, u32[]{:S(2)}) copy-start(f32[1,24576]{1,0:T(1,128)} %get-tuple-element.23) | copy-start | bytes 294916
  13.8 1.8 %copy-start.20 = (f32[1,24576]{1,0:T(1,128)S(1)}, f32[1,24576]{1,0:T(1,128)}, u32[]{:S(2)}) copy-start(f32[1,24576]{1,0:T(1,128)} %get-tuple-element.24) | copy-start | bytes 294916
  13.8 1.8 %copy-start.21 = (f32[1,24576]{1,0:T(1,128)S(1)}, f32[1,24576]{1,0:T(1,128)}, u32[]{:S(2)}) copy-start(f32[1,24576]{1,0:T(1,128)} %get-tuple-element.25) | copy-start | bytes 294916
  13.8 1.8 %copy-start.22 = (f32[1,24576]{1,0:T(1,128)S(1)}, f32[1,24576]{1,0:T(1,128)}, u32[]{:S(2)}) copy-start(f32[1,24576]{1,0:T(1,128)} %get-tuple-element.26) | copy-start | bytes 294916
  13.8 1.8 %copy-start.23 = (f32[1,24576]{1,0:T(1,128)S(1)}, f32[1,24576]{1,0:T(1,128)}, u32[]{:S(2)}) copy-start(f32[1,24576]{1,0:T(1,128)} %get-tuple-element.27) | copy-start | bytes 294916
  13.8 1.9 %copy-start.24 = (f32[1,24576]{1,0:T(1,128)S(1)}, f32[1,24576]{1,0:T(1,128)}, u32[]{:S(2)}) copy-start(f32[1,24576]{1,0:T(1,128)} %get-tuple-element.28) | copy-start | bytes 294916
  23.4 15.6 %collective-permute-start.1 = (bf16[24,1536]{1,0:T(8,128)(2,1)S(1)}, bf16[24,1536]{1,0:T(8,128)(2,1)S(1)}, u32[]{:S(2)}, u32[]{:S(2)}) collective-permute-start(bf16[24,1536]{1,0:T(8,128)(2,1)S(1)} %get-tuple-element.43), channel_id=1, source_target_pairs={{0,1},{1,0},{2,3},{3,2},{4,5},{5,4},{6,7},{7,6},{8,9},{9,8},{10,11... | collective-permute-start | bytes 221192 | tf_op jit(solution)/shard_map/ppermute | solution.py:18
  35.1 6.9 %collective-permute-start.2 = (bf16[24,1536]{1,0:T(8,128)(2,1)S(1)}, bf16[24,1536]{1,0:T(8,128)(2,1)S(1)}, u32[]{:S(2)}, u32[]{:S(2)}) collective-permute-start(bf16[24,1536]{1,0:T(8,128)(2,1)S(1)} %get-tuple-element.42), channel_id=1, source_target_pairs={{0,2},{1,3},{2,0},{3,1},{4,6},{5,7},{6,4},{7,5},{8,10},{9,11},{10,... | collective-permute-start | bytes 221192 | tf_op jit(solution)/shard_map/ppermute | solution.py:18
  37.4 4.6 %collective-permute-start.3 = (bf16[24,1536]{1,0:T(8,128)(2,1)S(1)}, bf16[24,1536]{1,0:T(8,128)(2,1)S(1)}, u32[]{:S(2)}, u32[]{:S(2)}) collective-permute-start(bf16[24,1536]{1,0:T(8,128)(2,1)S(1)} %get-tuple-element.41), channel_id=1, source_target_pairs={{0,3},{1,2},{2,1},{3,0},{4,7},{5,6},{6,5},{7,4},{8,11},{9,10},{10,... | collective-permute-start | bytes 221192 | tf_op jit(solution)/shard_map/ppermute | solution.py:18
  37.4 7.2 %collective-permute-start.4 = (bf16[24,1536]{1,0:T(8,128)(2,1)S(1)}, bf16[24,1536]{1,0:T(8,128)(2,1)S(1)}, u32[]{:S(2)}, u32[]{:S(2)}) collective-permute-start(bf16[24,1536]{1,0:T(8,128)(2,1)S(1)} %get-tuple-element.40), channel_id=1, source_target_pairs={{0,4},{1,5},{2,6},{3,7},{4,0},{5,1},{6,2},{7,3},{8,12},{9,13},{10,... | collective-permute-start | bytes 221192 | tf_op jit(solution)/shard_map/ppermute | solution.py:18
  39.0 7.1 %collective-permute-start.5 = (bf16[24,1536]{1,0:T(8,128)(2,1)S(1)}, bf16[24,1536]{1,0:T(8,128)(2,1)S(1)}, u32[]{:S(2)}, u32[]{:S(2)}) collective-permute-start(bf16[24,1536]{1,0:T(8,128)(2,1)S(1)} %get-tuple-element.39), channel_id=1, source_target_pairs={{0,5},{1,4},{2,7},{3,6},{4,1},{5,0},{6,3},{7,2},{8,13},{9,12},{10,... | collective-permute-start | bytes 221192 | tf_op jit(solution)/shard_map/ppermute | solution.py:18
  39.0 9.6 %collective-permute-start.6 = (bf16[24,1536]{1,0:T(8,128)(2,1)S(1)}, bf16[24,1536]{1,0:T(8,128)(2,1)S(1)}, u32[]{:S(2)}, u32[]{:S(2)}) collective-permute-start(bf16[24,1536]{1,0:T(8,128)(2,1)S(1)} %get-tuple-element.38), channel_id=1, source_target_pairs={{0,6},{1,7},{2,4},{3,5},{4,2},{5,3},{6,0},{7,1},{8,14},{9,15},{10,... | collective-permute-start | bytes 221192 | tf_op jit(solution)/shard_map/ppermute | solution.py:18
  42.0 7.2 %collective-permute-start.7 = (bf16[24,1536]{1,0:T(8,128)(2,1)S(1)}, bf16[24,1536]{1,0:T(8,128)(2,1)S(1)}, u32[]{:S(2)}, u32[]{:S(2)}) collective-permute-start(bf16[24,1536]{1,0:T(8,128)(2,1)S(1)} %get-tuple-element.37), channel_id=1, source_target_pairs={{0,7},{1,6},{2,5},{3,4},{4,3},{5,2},{6,1},{7,0},{8,15},{9,14},{10,... | collective-permute-start | bytes 221192 | tf_op jit(solution)/shard_map/ppermute | solution.py:18
  42.1 9.9 %collective-permute-start.8 = (bf16[24,1536]{1,0:T(8,128)(2,1)S(1)}, bf16[24,1536]{1,0:T(8,128)(2,1)S(1)}, u32[]{:S(2)}, u32[]{:S(2)}) collective-permute-start(bf16[24,1536]{1,0:T(8,128)(2,1)S(1)} %get-tuple-element.36), channel_id=1, source_target_pairs={{0,8},{1,9},{2,10},{3,11},{4,12},{5,13},{6,14},{7,15},{8,0},{9,1},... | collective-permute-start | bytes 221192 | tf_op jit(solution)/shard_map/ppermute | solution.py:18
  44.6 13.9 %collective-permute-start.9 = (bf16[24,1536]{1,0:T(8,128)(2,1)S(1)}, bf16[24,1536]{1,0:T(8,128)(2,1)S(1)}, u32[]{:S(2)}, u32[]{:S(2)}) collective-permute-start(bf16[24,1536]{1,0:T(8,128)(2,1)S(1)} %get-tuple-element.35), channel_id=1, source_target_pairs={{0,9},{1,8},{2,11},{3,10},{4,13},{5,12},{6,15},{7,14},{8,1},{9,0},... | collective-permute-start | bytes 221192 | tf_op jit(solution)/shard_map/ppermute | solution.py:18
  46.1 16.4 %collective-permute-start.10 = (bf16[24,1536]{1,0:T(8,128)(2,1)S(1)}, bf16[24,1536]{1,0:T(8,128)(2,1)S(1)}, u32[]{:S(2)}, u32[]{:S(2)}) collective-permute-start(bf16[24,1536]{1,0:T(8,128)(2,1)S(1)} %get-tuple-element.34), channel_id=1, source_target_pairs={{0,10},{1,11},{2,8},{3,9},{4,14},{5,15},{6,12},{7,13},{8,2},{9,3},... | collective-permute-start | bytes 221192 | tf_op jit(solution)/shard_map/ppermute | solution.py:18
  48.6 14.8 %collective-permute-start.11 = (bf16[24,1536]{1,0:T(8,128)(2,1)S(1)}, bf16[24,1536]{1,0:T(8,128)(2,1)S(1)}, u32[]{:S(2)}, u32[]{:S(2)}) collective-permute-start(bf16[24,1536]{1,0:T(8,128)(2,1)S(1)} %get-tuple-element.33), channel_id=1, source_target_pairs={{0,11},{1,10},{2,9},{3,8},{4,15},{5,14},{6,13},{7,12},{8,3},{9,2},... | collective-permute-start | bytes 221192 | tf_op jit(solution)/shard_map/ppermute | solution.py:18
  49.2 14.2 %collective-permute-start.12 = (bf16[24,1536]{1,0:T(8,128)(2,1)S(1)}, bf16[24,1536]{1,0:T(8,128)(2,1)S(1)}, u32[]{:S(2)}, u32[]{:S(2)}) collective-permute-start(bf16[24,1536]{1,0:T(8,128)(2,1)S(1)} %get-tuple-element.32), channel_id=1, source_target_pairs={{0,12},{1,13},{2,14},{3,15},{4,8},{5,9},{6,10},{7,11},{8,4},{9,5},... | collective-permute-start | bytes 221192 | tf_op jit(solution)/shard_map/ppermute | solution.py:18
  52.0 11.5 %collective-permute-start.13 = (bf16[24,1536]{1,0:T(8,128)(2,1)S(1)}, bf16[24,1536]{1,0:T(8,128)(2,1)S(1)}, u32[]{:S(2)}, u32[]{:S(2)}) collective-permute-start(bf16[24,1536]{1,0:T(8,128)(2,1)S(1)} %get-tuple-element.31), channel_id=1, source_target_pairs={{0,13},{1,12},{2,15},{3,14},{4,9},{5,8},{6,11},{7,10},{8,5},{9,4},... | collective-permute-start | bytes 221192 | tf_op jit(solution)/shard_map/ppermute | solution.py:18
  58.6 7.2 %collective-permute-start.14 = (bf16[24,1536]{1,0:T(8,128)(2,1)S(1)}, bf16[24,1536]{1,0:T(8,128)(2,1)S(1)}, u32[]{:S(2)}, u32[]{:S(2)}) collective-permute-start(bf16[24,1536]{1,0:T(8,128)(2,1)S(1)} %get-tuple-element.30), channel_id=1, source_target_pairs={{0,14},{1,15},{2,12},{3,13},{4,10},{5,11},{6,8},{7,9},{8,6},{9,7},... | collective-permute-start | bytes 221192 | tf_op jit(solution)/shard_map/ppermute | solution.py:18
  62.5 7.2 %collective-permute-start.15 = (bf16[24,1536]{1,0:T(8,128)(2,1)S(1)}, bf16[24,1536]{1,0:T(8,128)(2,1)S(1)}, u32[]{:S(2)}, u32[]{:S(2)}) collective-permute-start(bf16[24,1536]{1,0:T(8,128)(2,1)S(1)} %get-tuple-element.29), channel_id=1, source_target_pairs={{0,15},{1,14},{2,13},{3,12},{4,11},{5,10},{6,9},{7,8},{8,7},{9,6},... | collective-permute-start | bytes 221192 | tf_op jit(solution)/shard_map/ppermute | solution.py:18
Sparse Core Ops, SparseCore 0:
  78.0 71.2 reduce-scatter.3
